TPU v7x, 32 devices: a whole 2x2x4 slice. The times are simulated.
32 devices in a mesh: gx: 16 (over z, x, core), yz: 2 (over y).
Axes of the slice: x: 2, y: 2, z: 4, core: 2. Of those that a mesh axis runs over, the one named last changes fastest.
Arguments:
- conformation: float32 [3, 64, 384, 1024], P(None, 'gx', 'yz'), may hold values from -0.49 to 2.5, as said below
- velocity: float32 [3, 64, 384, 1024], P(None, 'gx', 'yz'), may hold values from -6 to 6
Outputs:
- updated: float32 [3, 64, 384, 1024], P(None, 'gx', 'yz')
Inputs may be any that keep to these rules, and one draw needn't show every extreme that they name: `conformation`: components 0 and 2 (c_xx, c_yy) lie in [0.5, 2.5] and component 1 (c_xy) in [-0.49, 0.49].
All inputs are finite; a program needn't handle non-finite values.
Results may differ from a plain program's by a relative error of at most 0.000076.
Values sent between devices are 32-bit elements; how exact they have to be, the bound alone decides.
No kernel may reach another device: no remote copies, remote signals or barrier semaphores. Data moves between devices by JAX's collectives and lax.ppermute only.
A program may use at most 256 MiB of HBM per device.

v0:
```python
import math
import jax
import jax.numpy as jnp
from jax import lax
from jax.sharding import PartitionSpec as P

stencil_coeffs = (0.8, -0.2, 4.0 / 105.0, -1.0 / 280.0)
extensibility = 10.0
relax_rate = 1.0 / 0.04
courant = 0.5


def padded_2(x, sides, width):
    for axis, dim in sides:
        count, length = (lax.axis_size(axis), x.shape[dim])
        up = [(i, (i + 1) % count) for i in range(count)]
        down = [(j, i) for i, j in up]
        last = lax.slice_in_dim(x, length - width, length, axis=dim)
        initial = lax.slice_in_dim(x, 0, width, axis=dim)
        before = lax.ppermute(last, axis, up)
        after = lax.ppermute(initial, axis, down)
        x = jnp.concatenate([before, x, after], axis=dim)
    return x


def storage_points(count, groups):
    index = jnp.arange(count, dtype=jnp.int32)
    per_group = count // groups
    return index % per_group * groups + index // per_group


def cheb_matrix(count, points):
    last = count - 1
    half_step = math.pi / (2.0 * last)
    weights = jnp.where((points == 0) | (points == last), 2.0, 1.0).astype(jnp.float32)
    same = points[:, None] == points[None, :]
    sums = (points[:, None] + points[None, :]).astype(jnp.float32) * half_step
    diffs = (points[:, None] - points[None, :]).astype(jnp.float32) * half_step
    signs = (1 - 2 * ((points[:, None] + points[None, :]) % 2)).astype(jnp.float32)
    apart = -2.0 * jnp.sin(sums) * jnp.sin(diffs)
    safe = jnp.where(same, 1.0, apart)
    offdiag = jnp.where(same, 0.0, weights[:, None] / weights[None, :] * signs / safe)
    return offdiag - jnp.diag(jnp.sum(offdiag, axis=1))


def centered(padded, width, count, axis, spacing):
    total = jnp.zeros_like(lax.slice_in_dim(padded, width, width + count, axis=axis))
    for offset, coeff in enumerate(stencil_coeffs, start=1):
        ahead = lax.slice_in_dim(padded, width + offset, width + offset + count, axis=axis)
        behind = lax.slice_in_dim(padded, width - offset, width - offset + count, axis=axis)
        total = total + coeff * (ahead - behind)
    return total / spacing


def wall_terms(comp, vel_v, dy_comp, dy_u, dy_v):
    term_xx = -vel_v * dy_comp[0] + 2.0 * dy_u * comp[1]
    term_xy = -vel_v * dy_comp[1] + dy_u * comp[2] + dy_v * comp[1]
    term_yy = -vel_v * dy_comp[2] + 2.0 * dy_v * comp[2]
    return jnp.stack([term_xx, term_xy, term_yy])


def local_terms(comp, vel, along_x, along_z):
    peterlin = (extensibility - 2.0) / (extensibility - comp[0] - comp[2])
    grad_ux = along_x[3]
    grad_vx = along_x[4]
    term_xx = (
        -vel[0] * along_x[0]
        - vel[2] * along_z[0]
        + 2.0 * grad_ux * comp[0]
        - relax_rate * (peterlin * comp[0] - 1.0)
    )
    term_xy = (
        -vel[0] * along_x[1]
        - vel[2] * along_z[1]
        + grad_ux * comp[1]
        + grad_vx * comp[0]
        - relax_rate * peterlin * comp[1]
    )
    term_yy = (
        -vel[0] * along_x[2]
        - vel[2] * along_z[2]
        + 2.0 * grad_vx * comp[1]
        - relax_rate * (peterlin * comp[2] - 1.0)
    )
    return jnp.stack([term_xx, term_xy, term_yy])


def shards(conformation, velocity):
    planes = conformation.shape[1]
    local_rows = conformation.shape[2]
    groups = lax.axis_size("yz")
    count = local_rows * groups
    spacing = math.pi / (count - 1)
    points = storage_points(count, groups)
    cheb = cheb_matrix(count, points)
    points_here = jnp.arange(local_rows, dtype=jnp.int32) * groups + lax.axis_index("yz")
    theta = math.pi * points_here.astype(jnp.float32) / (count - 1)
    step_size = courant * spacing * (jnp.sin(theta) + spacing)
    block = jnp.concatenate([conformation, velocity[0:2]], axis=0)
    derived = jnp.einsum(
        "ij,fkjz->fkiz",
        cheb,
        lax.all_to_all(block, "yz", split_axis=3, concat_axis=2, tiled=True),
        precision=lax.Precision.HIGHEST,
    )
    returned_back = lax.all_to_all(derived, "yz", split_axis=2, concat_axis=3, tiled=True)
    yterms = wall_terms(
        conformation, velocity[1], returned_back[0:3], returned_back[3], returned_back[4]
    )
    padded = padded_2(block, (("gx", 1),), 4)
    along_x = centered(padded, 4, planes, 1, spacing)
    padded_z = jnp.pad(conformation, ((0, 0), (0, 0), (0, 0), (4, 4)), mode="wrap")
    along_z = centered(padded_z, 4, conformation.shape[3], 3, spacing)
    other = local_terms(conformation, velocity, along_x, along_z)
    return conformation + step_size[None, None, :, None] * (other + yterms)


def solution(mesh):
    in_specs = (P(None, "gx", "yz", None), P(None, "gx", "yz", None))
    out_specs = P(None, "gx", "yz", None)
    return jax.shard_map(shards, mesh=mesh, in_specs=in_specs, out_specs=out_specs, check_vma=False)
```

profile of v0, /device:TPU:16, one launch (start us, length us, event | category | flops | bytes accessed | tf_op | source)
XLA Modules:
  0.0 632.3 jit_solution(1645302906625651038)
XLA Ops:
  0.0 0.0 copy-start
  0.0 3.5 slice.149
  3.5 2.0 copy-done
  5.5 0.0 copy-start.2
  5.5 6.6 %pad_maximum_fusion.1 = f32[5,4,192,1024]{3,2,1,0:T(8,128)} fusion(f32[2,4,192,1024]{3,2,1,0:T(8,128)S(1)} %slice.149, f32[3,4,192,1024]{3,2,1,0:T(8,128)S(1)} %copy-done), kind=kLoop, calls=%fused_computation.18 | loop fusion | flops 3932160 | bytes 31457280 | tf_op jit(solution)/shard_map/concatenate | solution.py:99
  12.1 0.8 copy-done.2
  12.9 0.8 collective-permute-start
  13.7 0.0 collective-permute-start.1
  13.7 21.9 %copy.19 = f32[5,4,192,1024]{2,1,0,3:T(4,128)} copy(f32[5,4,192,1024]{3,2,1,0:T(8,128)} %pad_maximum_fusion.1) | data formatting | bytes 31457280 | tf_op jit(solution)/shard_map/concatenate | solution.py:99
  35.6 11.2 %all-to-all-start = ((f32[5,4,192,1024]{2,1,0,3:T(4,128)}), f32[5,4,192,1024]{2,1,0,3:T(4,128)}, u32[]{:S(2)}, u32[]{:S(2)}) async-start(f32[5,4,192,1024]{2,1,0,3:T(4,128)} %copy.19), calls=%async_computation | async-start | bytes 41943040 | tf_op jit(solution)/shard_map/all_to_all | solution.py:103
  46.8 0.6 add_multiply_fusion
  47.5 2.0 fusion.68
  49.5 4.8 fusion.51
  54.3 4.4 fusion.73
  58.8 36.0 %fusion.12 = f32[3,4,192,1024]{3,2,1,0:T(8,128)} fusion(f32[3,4,192,1024]{3,2,1,0:T(8,128)} %param.2, f32[3,4,192,4]{3,2,1,0:T(8,128)S(1)} %get-tuple-element.18, f32[3,4,192,4]{3,2,1,0:T(8,128)S(1)} %get-tuple-element.17), kind=kLoop, calls=%fused_computation.30 | loop fusion | flops 47185920 | bytes 18948096 | tf_op jit(solution)/shard_map/div | solution.py:52
  94.8 180.4 %all-to-all-done = f32[5,4,192,1024]{2,1,0,3:T(4,128)} async-done(((f32[5,4,192,1024]{2,1,0,3:T(4,128)}), f32[5,4,192,1024]{2,1,0,3:T(4,128)}, u32[]{:S(2)}, u32[]{:S(2)}) %all-to-all-start) | async-done | bytes 15728672 | tf_op jit(solution)/shard_map/all_to_all | solution.py:103
  275.2 30.9 %copy.32 = f32[5,4,192,2,512]{4,3,2,1,0:T(2,128)} copy(f32[5,4,192,2,512]{2,1,0,4,3:T(4,128)} %bitcast) | data formatting | bytes 31457280 | tf_op jit(solution)/shard_map/all_to_all | solution.py:103
  306.2 14.0 %copy.21 = f32[5,4,2,192,512]{4,3,2,1,0:T(8,128)} copy(f32[5,4,2,192,512]{4,2,3,1,0:T(2,128)} %bitcast.39) | data formatting | bytes 31457280 | tf_op jit(solution)/shard_map/all_to_all | solution.py:103
  320.1 54.5 %convolution_bitcast_fusion = f32[5,4,384,512]{2,3,1,0:T(8,128)} fusion(f32[5,4,384,512]{3,2,1,0:T(8,128)} %bitcast.38, f32[384,384,1,1]{1,0,3,2:T(8,128)S(1)} %fusion.73), kind=kOutput, calls=%fused_computation.48 | convolution fusion | flops 18119393280 | bytes 32047104 | tf_op jit(solution)/shard_map/ij,fkjz->fkiz/dot_general | solution.py:100
  374.6 19.4 %copy.23 = f32[5,4,384,512]{3,1,0,2:T(4,128)} copy(f32[5,4,384,512]{2,3,1,0:T(8,128)} %convolution_bitcast_fusion) | data formatting | bytes 31457280 | tf_op jit(solution)/shard_map/ij,fkjz->fkiz/transpose | solution.py:100
  394.1 9.4 %all-to-all-start.1 = ((f32[5,4,384,512]{3,1,0,2:T(4,128)}), f32[5,4,384,512]{3,1,0,2:T(4,128)}, u32[]{:S(2)}, u32[]{:S(2)}) async-start(f32[5,4,384,512]{3,1,0,2:T(4,128)} %copy.23), calls=%async_computation.1 | async-start | bytes 31457280 | tf_op jit(solution)/shard_map/all_to_all | solution.py:106
  403.5 0.0 collective-permute-done
  403.5 0.0 collective-permute-done.1
  403.5 41.9 %pad_maximum_fusion = (f32[5,8,192,1024]{3,2,1,0:T(8,128)}, f32[5,8,192,1024]{3,2,1,0:T(8,128)}) fusion(f32[5,4,192,1024]{3,2,1,0:T(8,128)} %collective-permute-done, f32[2,4,192,1024]{3,2,1,0:T(8,128)} %copy-done.2, f32[3,4,192,1024]{3,2,1,0:T(8,128)} %param.2, f32[5,4,192,1024]{3,2,1,0:T(8,128)} %collective-permute-done.1), kind=kLoop, calls=%fused_computation | loop fusion | flops 31457280 | bytes 110100480 | tf_op jit(solution)/shard_map/concatenate | solution.py:22
  445.4 46.8 %fusion.3 = f32[5,4,192,1024]{3,2,1,0:T(8,128)} fusion(f32[5,8,192,1024]{3,2,1,0:T(8,128)} %get-tuple-element.16, f32[5,8,192,1024]{3,2,1,0:T(8,128)} %get-tuple-element.15, f32[5,4,192,1024]{3,2,1,0:T(8,128)} %collective-permute-done, f32[5,4,192,1024]{3,2,1,0:T(8,128)} %collective-permute-done.1), kind=kLoop, calls=%fused_computation.12 | loop fusion | flops 47185920 | bytes 141557760 | tf_op jit(solution)/shard_map/div | solution.py:52
  492.3 0.0 copy-start.1
  492.3 13.0 %fusion.33 = f32[1,4,192,1024]{3,2,1,0:T(8,128)} fusion(f32[3,4,192,1024]{3,2,1,0:T(8,128)} %fusion.12, f32[5,4,192,1024]{3,2,1,0:T(8,128)} %fusion.3, f32[3,4,192,1024]{3,2,1,0:T(8,128)} %param.2, f32[3,4,192,1024]{3,2,1,0:T(8,128)} %param.3), kind=kLoop, calls=%fused_computation.63 | loop fusion | flops 11010048 | bytes 31457280 | tf_op jit(solution)/shard_map/sub | solution.py:73
  505.2 1.8 copy-done.1
  507.0 11.3 %fusion.36 = (f32[1,4,192,1024]{3,2,1,0:T(8,128)}, f32[1,4,192,1024]{3,2,1,0:T(8,128)}) fusion(f32[3,4,192,1024]{3,2,1,0:T(8,128)} %fusion.12, f32[5,4,192,1024]{3,2,1,0:T(8,128)S(1)} %copy-done.1, f32[3,4,192,1024]{3,2,1,0:T(8,128)} %param.2, f32[3,4,192,1024]{3,2,1,0:T(8,128)} %param.3), kind=kLoop, calls=%fused_computation.68 | loop fusion | flops 18874368 | bytes 40894464 | tf_op jit(solution)/shard_map/sub | solution.py:67
  518.3 56.5 %all-to-all-done.1 = f32[5,4,384,512]{3,1,0,2:T(4,128)} async-done(((f32[5,4,384,512]{3,1,0,2:T(4,128)}), f32[5,4,384,512]{3,1,0,2:T(4,128)}, u32[]{:S(2)}, u32[]{:S(2)}) %all-to-all-start.1) | async-done | bytes 15728672 | tf_op jit(solution)/shard_map/all_to_all | solution.py:106
  574.9 15.8 %copy.24 = f32[5,4,384,512]{3,2,1,0:T(8,128)} copy(f32[5,4,384,512]{3,1,0,2:T(4,128)} %all-to-all-done.1) | data formatting | bytes 31457280 | tf_op jit(solution)/shard_map/all_to_all | solution.py:106
  590.7 11.9 %slice_bitcast_fusion.4 = (f32[1,4,2,24,8,512]{5,4,3,2,1,0:T(8,128)}, f32[1,4,2,24,8,512]{5,4,3,2,1,0:T(8,128)}, f32[1,4,2,24,8,512]{5,4,3,2,1,0:T(8,128)}, f32[...) fusion(f32[5,4,192,2,512]{4,2,3,1,0:T(8,128)} %bitcast.37), kind=kLoop, calls=%fused_computation.53 | loop fusion | bytes 31457280
  602.6 0.0 copy-start.4
  602.6 2.4 copy.33
  605.0 0.0 copy-start.3
  605.0 0.0 slice-start
  605.0 2.4 copy.34
  607.4 0.0 slice-start.1
  607.4 0.4 copy.35
  607.8 0.0 copy-done.4
  607.8 0.0 slice-start.2
  607.8 0.4 copy.36
  608.2 0.0 copy-done.3
  608.2 2.0 copy.37
  610.1 0.0 slice-done
  610.1 1.4 slice-done.1
  611.6 0.2 slice-done.2
  611.8 0.0 copy-start.5
  611.8 8.3 %multiply_add_fusion.2 = (f32[1,4,192,1024]{3,2,1,0:T(8,128)}, f32[1,4,192,1024]{3,2,1,0:T(8,128)}, f32[1,4,192,1024]{3,2,1,0:T(8,128)}) fusion(f32[1,4,192,1024]{3,2,1,0:T(8,128)S(1)} %bitcast.41, f32[1,4,192,1024]{3,2,1,0:T(8,128)S(1)} %bitcast.40, f32[3,4,192,1024]{3,2,1,0:T(8,128)S(1)} %bitcast.36, f32[3,4,192,1024]{3,2,1,0:T(8,128)} %param.3, ...), kind=kLoop, calls=%fused_computation.72 | loop fusion | flops 11010048 | bytes 34603008 | tf_op jit(solution)/shard_map/add | solution.py:56
  620.1 0.0 copy-done.5
  620.1 11.9 %fusion.26 = f32[3,4,192,1024]{3,2,1,0:T(8,128)} fusion(f32[3,4,192,1024]{3,2,1,0:T(8,128)S(1)} %bitcast.36, f32[1,4,192,1024]{3,2,1,0:T(8,128)} %get-tuple-element.6, f32[1,4,192,1024]{3,2,1,0:T(8,128)} %fusion.33, f32[1,4,192,1024]{3,2,1,0:T(8,128)} %get-tuple-element.5, f32[1,4,192,1024]{3,2,1,0:T(8,128)} %get-tuple-element.9, ...), kind=kLoop, calls=%fused_computation.47 | loop fusion | flops 16515072 | bytes 37749504 | tf_op jit(solution)/shard_map/add | solution.py:115
  (3 shorter events, 0.0 us)
Async XLA Ops:
  0.0 5.5 copy-start
  5.5 7.4 %copy-start.2 = (f32[2,4,192,1024]{3,2,1,0:T(8,128)}, f32[2,4,192,1024]{3,2,1,0:T(8,128)S(1)}, u32[]{:S(2)}) copy-start(f32[2,4,192,1024]{3,2,1,0:T(8,128)S(1)} %slice.149) | copy-start | bytes 18874372
  12.9 390.6 %collective-permute-start = (f32[5,4,192,1024]{3,2,1,0:T(8,128)}, f32[5,4,192,1024]{3,2,1,0:T(8,128)}, u32[]{:S(2)}, u32[]{:S(2)}) collective-permute-start(f32[5,4,192,1024]{3,2,1,0:T(8,128)} %pad_maximum_fusion.1), channel_id=1, source_target_pairs={{2,0},{4,2},{6,4},{8,6},{10,8},{12,10},{14,12},{16,14},{18,16},{20... | collective-permute-start | bytes 47185928 | tf_op jit(solution)/shard_map/ppermute | solution.py:21
  13.7 389.8 %collective-permute-start.1 = (f32[5,4,192,1024]{3,2,1,0:T(8,128)}, f32[5,4,192,1024]{3,2,1,0:T(8,128)}, u32[]{:S(2)}, u32[]{:S(2)}) collective-permute-start(f32[5,4,192,1024]{3,2,1,0:T(8,128)} %pad_maximum_fusion.1), channel_id=1, source_target_pairs={{0,2},{2,4},{4,6},{6,8},{8,10},{10,12},{12,14},{14,16},{16,18},{18... | collective-permute-start | bytes 47185928 | tf_op jit(solution)/shard_map/ppermute | solution.py:20
  35.6 239.6 %all-to-all-start = ((f32[5,4,192,1024]{2,1,0,3:T(4,128)}), f32[5,4,192,1024]{2,1,0,3:T(4,128)}, u32[]{:S(2)}, u32[]{:S(2)}) async-start(f32[5,4,192,1024]{2,1,0,3:T(4,128)} %copy.19), calls=%async_computation | async-start | bytes 41943040 | tf_op jit(solution)/shard_map/all_to_all | solution.py:103
  394.1 180.8 %all-to-all-start.1 = ((f32[5,4,384,512]{3,1,0,2:T(4,128)}), f32[5,4,384,512]{3,1,0,2:T(4,128)}, u32[]{:S(2)}, u32[]{:S(2)}) async-start(f32[5,4,384,512]{3,1,0,2:T(4,128)} %copy.23), calls=%async_computation.1 | async-start | bytes 31457280 | tf_op jit(solution)/shard_map/all_to_all | solution.py:106
  492.3 14.7 %copy-start.1 = (f32[5,4,192,1024]{3,2,1,0:T(8,128)S(1)}, f32[5,4,192,1024]{3,2,1,0:T(8,128)}, u32[]{:S(2)}) copy-start(f32[5,4,192,1024]{3,2,1,0:T(8,128)} %fusion.3) | copy-start | bytes 47185924
  602.6 5.2 copy-start.4
  605.0 3.2 copy-start.3
  605.0 5.2 slice-start
  607.4 4.2 slice-start.1
  607.8 4.0 slice-start.2
  611.8 8.4 %copy-start.5 = (f32[192]{0:T(256)S(1)}, f32[192]{0:T(256)}, u32[]{:S(2)}) copy-start(f32[192]{0:T(256)} %add_multiply_fusion) | copy-start | bytes 2308
where the time goes:
time: 641 us; the launch traced here: 632 us
  waiting for transfers between devices  237 us (37%)
  other arithmetic  186 us (29%)
  local copies, waits for them, and re-layouts  133 us (21%)
  matrix products  54.5 us (9%)
  starting transfers between devices  21.4 us (3%)
    all_to_all x1, waiting for transfers between devices, shards(): lax.all_to_all(block, 'yz', split_axis=3, concat_axis=2, tiled=True)  180 us
    div x2, other arithmetic, centered(): return total / spacing  82.8 us
    all_to_all x1, waiting for transfers between devices, shards(): lax.all_to_all(derived, 'yz', split_axis=2, concat_axis=3, tiled=True)  56.5 us
    dot_general x1, matrix products, shards(): jnp.einsum('ij,fkjz->fkiz', cheb, lax.all_to_all(block, 'yz', split_axis=...  54.5 us
    all_to_all x2, local copies, waits for them, and re-layouts, shards(): lax.all_to_all(block, 'yz', split_axis=3, concat_axis=2, tiled=True)  44.9 us
    concatenate x1, other arithmetic, padded_2(): x = jnp.concatenate([before, x, after], axis=dim)  41.9 us
    concatenate x1, local copies, waits for them, and re-layouts, shards(): block = jnp.concatenate([conformation, velocity[0:2]], axis=0)  21.9 us
    transpose x1, local copies, waits for them, and re-layouts, shards(): jnp.einsum('ij,fkjz->fkiz', cheb, lax.all_to_all(block, 'yz', split_axis=...  19.4 us
  transfers between devices with their start and end apart: 4, of which 2 were waited for; matrix products, arithmetic and copies ran while one was open for 48% of the time, Pallas kernels for 0%

commit v1 on v0

--- a/solution.py
+++ b/solution.py
@@ -8,6 +8,13 @@
 extensibility = 10.0
 relax_rate = 1.0 / 0.04
 courant = 0.5
+
+
+def trade_parts(block, name, split, join):
+    size = lax.axis_size(name)
+    blocks = jnp.stack(jnp.split(block, size, axis=split), axis=0)
+    blocks = lax.all_to_all(blocks, name, split_axis=0, concat_axis=0)
+    return jnp.concatenate(blocks, axis=join)
 
 
 def padded_2(x, sides, width):
@@ -103,7 +110,7 @@
         lax.all_to_all(block, "yz", split_axis=3, concat_axis=2, tiled=True),
         precision=lax.Precision.HIGHEST,
     )
-    returned_back = lax.all_to_all(derived, "yz", split_axis=2, concat_axis=3, tiled=True)
+    returned_back = trade_parts(derived, "yz", 2, 3)
     yterms = wall_terms(
         conformation, velocity[1], returned_back[0:3], returned_back[3], returned_back[4]
     )

time: 641 us -> 599 us (0.934)
  local copies, waits for them, and re-layouts: 133 us -> 89.5 us
  matrix products: 54.5 us -> 41.9 us
  other arithmetic: 186 us -> 195 us
    all_to_all x2 -> x1, local copies, waits for them, and re-layouts: 44.9 us -> 22.2 us  [shards(): lax.all_to_all(block, 'yz', split_axis=3, concat_axis=2, tiled=True)]
    transpose x1 -> x0, local copies, waits for them, and re-layouts: 19.4 us -> none  [shards(): jnp.einsum('ij,fkjz->fkiz', cheb, lax.all_to_all(block, 'yz', split_axis=...]
    all_to_all x1 -> x0, local copies, waits for them, and re-layouts: 15.8 us -> none  [shards(): lax.all_to_all(derived, 'yz', split_axis=2, concat_axis=3, tiled=True)]
    another operation x0 -> x1, local copies, waits for them, and re-layouts: none -> 14.3 us  [trade_parts(): blocks = jnp.stack(jnp.split(block, size, axis=split), axis=0)]
    another operation x0 -> x1, other arithmetic: none -> 14.3 us  [trade_parts(): blocks = jnp.stack(jnp.split(block, size, axis=split), axis=0)]
    dot_general x1, matrix products: 54.5 us -> 41.9 us  [shards(): jnp.einsum('ij,fkjz->fkiz', cheb, lax.all_to_all(block, 'yz', split_axis=...]
  transfers between devices with their start and end apart: 4 -> 4, of which waited for: 2 -> 2; matrix products, arithmetic and copies ran while one was open for 48% -> 46% of each run, Pallas kernels for 0% -> 0%
where the time goes in v1:
time: 599 us; the launch traced here: 590 us
  waiting for transfers between devices  242 us (40%)
  other arithmetic  195 us (33%)
  local copies, waits for them, and re-layouts  89.5 us (15%)
  matrix products  41.9 us (7%)
  starting transfers between devices  21.5 us (4%)
    all_to_all x1, waiting for transfers between devices, shards(): lax.all_to_all(block, 'yz', split_axis=3, concat_axis=2, tiled=True)  185 us
    div x2, other arithmetic, centered(): return total / spacing  82.7 us
    all_to_all x1, waiting for transfers between devices, trade_parts(): blocks = lax.all_to_all(blocks, name, split_axis=0, concat_axis=0)  56.7 us
    dot_general x1, matrix products, shards(): jnp.einsum('ij,fkjz->fkiz', cheb, lax.all_to_all(block, 'yz', split_axis=...  41.9 us
    concatenate x1, other arithmetic, padded_2(): x = jnp.concatenate([before, x, after], axis=dim)  41.7 us
    all_to_all x1, local copies, waits for them, and re-layouts, shards(): lax.all_to_all(block, 'yz', split_axis=3, concat_axis=2, tiled=True)  22.2 us
    concatenate x1, local copies, waits for them, and re-layouts, shards(): block = jnp.concatenate([conformation, velocity[0:2]], axis=0)  21.8 us
    unnamed x19, local copies, waits for them, and re-layouts  18.2 us
  transfers between devices with their start and end apart: 4, of which 2 were waited for; matrix products, arithmetic and copies ran while one was open for 46% of the time, Pallas kernels for 0%

profile of v1, /device:TPU:16, one launch (start us, length us, event | category | flops | bytes accessed | tf_op | source)
XLA Modules:
  0.0 590.2 jit_solution(8818032292267541309)
XLA Ops:
  0.0 0.0 copy-start
  0.0 3.5 slice.149
  3.5 2.0 copy-done
  5.5 0.0 copy-start.2
  5.5 6.6 %pad_maximum_fusion.1 = f32[5,4,192,1024]{3,2,1,0:T(8,128)} fusion(f32[2,4,192,1024]{3,2,1,0:T(8,128)S(1)} %slice.149, f32[3,4,192,1024]{3,2,1,0:T(8,128)S(1)} %copy-done), kind=kLoop, calls=%fused_computation.18 | loop fusion | flops 3932160 | bytes 31457280 | tf_op jit(solution)/shard_map/concatenate | solution.py:106
  12.1 0.8 copy-done.2
  12.9 0.8 collective-permute-start
  13.7 0.0 collective-permute-start.1
  13.7 21.8 %copy.10 = f32[5,4,192,1024]{2,1,0,3:T(4,128)} copy(f32[5,4,192,1024]{3,2,1,0:T(8,128)} %pad_maximum_fusion.1) | data formatting | bytes 31457280 | tf_op jit(solution)/shard_map/concatenate | solution.py:106
  35.5 11.2 %all-to-all-start = ((f32[5,4,192,1024]{2,1,0,3:T(4,128)}), f32[5,4,192,1024]{2,1,0,3:T(4,128)}, u32[]{:S(2)}, u32[]{:S(2)}) async-start(f32[5,4,192,1024]{2,1,0,3:T(4,128)} %copy.10), calls=%async_computation | async-start | bytes 41943040 | tf_op jit(solution)/shard_map/all_to_all | solution.py:110
  46.7 0.6 add_multiply_fusion
  47.3 2.0 fusion.68
  49.3 4.8 fusion.51
  54.2 35.8 %fusion.12 = f32[3,4,192,1024]{3,2,1,0:T(8,128)} fusion(f32[3,4,192,1024]{3,2,1,0:T(8,128)} %param.2, f32[3,4,192,4]{3,2,1,0:T(8,128)S(1)} %get-tuple-element.20, f32[3,4,192,4]{3,2,1,0:T(8,128)S(1)} %get-tuple-element.19), kind=kLoop, calls=%fused_computation.31 | loop fusion | flops 47185920 | bytes 18948096 | tf_op jit(solution)/shard_map/div | solution.py:59
  90.0 185.1 %all-to-all-done = f32[5,4,192,1024]{2,1,0,3:T(4,128)} async-done(((f32[5,4,192,1024]{2,1,0,3:T(4,128)}), f32[5,4,192,1024]{2,1,0,3:T(4,128)}, u32[]{:S(2)}, u32[]{:S(2)}) %all-to-all-start) | async-done | bytes 15728672 | tf_op jit(solution)/shard_map/all_to_all | solution.py:110
  275.1 22.2 %copy.11 = f32[5,4,192,2,512]{4,2,3,1,0:T(8,128)} copy(f32[5,4,192,2,512]{2,1,0,4,3:T(4,128)} %bitcast) | data formatting | bytes 31457280 | tf_op jit(solution)/shard_map/all_to_all | solution.py:110
  297.2 41.9 %convolution_bitcast_fusion = f32[5,4,384,512]{3,2,1,0:T(8,128)} fusion(f32[5,4,384,512]{3,2,1,0:T(8,128)} %bitcast.34, f32[384]{0:T(512)S(1)} %fusion.51, f32[384]{0:T(512)S(1)} %or_select_fusion, s32[384]{0:T(512)S(1)} %fusion.56), kind=kOutput, calls=%fused_computation.49 | convolution fusion | flops 18123964416 | bytes 31461888 | tf_op jit(solution)/shard_map/ij,fkjz->fkiz/dot_general | solution.py:107
  339.1 14.3 %slice_bitcast_fusion.1 = (f32[1,5,4,192,512]{4,3,2,1,0:T(8,128)}, f32[1,5,4,192,512]{4,3,2,1,0:T(8,128)}) fusion(f32[5,4,384,512]{3,2,1,0:T(8,128)} %convolution_bitcast_fusion), kind=kLoop, calls=%fused_computation.51 | loop fusion | bytes 31457280 | tf_op jit(solution)/shard_map/stack | solution.py:15
  353.5 14.3 %pad_maximum_fusion.2 = f32[2,5,4,192,512]{4,3,2,1,0:T(8,128)} fusion(f32[1,5,4,192,512]{4,3,2,1,0:T(8,128)} %get-tuple-element.16, f32[1,5,4,192,512]{4,3,2,1,0:T(8,128)} %get-tuple-element.15), kind=kLoop, calls=%fused_computation.19 | loop fusion | flops 3932160 | bytes 31457280 | tf_op jit(solution)/shard_map/stack | solution.py:15
  367.8 9.5 %all-to-all-start.1 = ((f32[2,5,4,192,512]{4,3,2,1,0:T(8,128)}), f32[2,5,4,192,512]{4,3,2,1,0:T(8,128)}, u32[]{:S(2)}, u32[]{:S(2)}) async-start(f32[2,5,4,192,512]{4,3,2,1,0:T(8,128)} %pad_maximum_fusion.2), calls=%async_computation.1 | async-start | bytes 31457280 | tf_op jit(solution)/shard_map/all_to_all | solution.py:16
  377.3 0.0 collective-permute-done
  377.3 0.0 collective-permute-done.1
  377.3 41.7 %pad_maximum_fusion = (f32[5,8,192,1024]{3,2,1,0:T(8,128)}, f32[5,8,192,1024]{3,2,1,0:T(8,128)}) fusion(f32[5,4,192,1024]{3,2,1,0:T(8,128)} %collective-permute-done, f32[2,4,192,1024]{3,2,1,0:T(8,128)} %copy-done.2, f32[3,4,192,1024]{3,2,1,0:T(8,128)} %param.2, f32[5,4,192,1024]{3,2,1,0:T(8,128)} %collective-permute-done.1), kind=kLoop, calls=%fused_computation | loop fusion | flops 31457280 | bytes 110100480 | tf_op jit(solution)/shard_map/concatenate | solution.py:29
  419.0 46.8 %fusion.3 = f32[5,4,192,1024]{3,2,1,0:T(8,128)} fusion(f32[5,8,192,1024]{3,2,1,0:T(8,128)} %get-tuple-element.18, f32[5,8,192,1024]{3,2,1,0:T(8,128)} %get-tuple-element.17, f32[5,4,192,1024]{3,2,1,0:T(8,128)} %collective-permute-done, f32[5,4,192,1024]{3,2,1,0:T(8,128)} %collective-permute-done.1), kind=kLoop, calls=%fused_computation.12 | loop fusion | flops 47185920 | bytes 141557760 | tf_op jit(solution)/shard_map/div | solution.py:59
  465.8 0.0 copy-start.1
  465.8 12.9 %fusion.33 = f32[1,4,192,1024]{3,2,1,0:T(8,128)} fusion(f32[3,4,192,1024]{3,2,1,0:T(8,128)} %fusion.12, f32[5,4,192,1024]{3,2,1,0:T(8,128)} %fusion.3, f32[3,4,192,1024]{3,2,1,0:T(8,128)} %param.2, f32[3,4,192,1024]{3,2,1,0:T(8,128)} %param.3), kind=kLoop, calls=%fused_computation.66 | loop fusion | flops 11010048 | bytes 31457280 | tf_op jit(solution)/shard_map/sub | solution.py:80
  478.7 1.8 copy-done.1
  480.5 11.4 %fusion.36 = (f32[1,4,192,1024]{3,2,1,0:T(8,128)}, f32[1,4,192,1024]{3,2,1,0:T(8,128)}) fusion(f32[3,4,192,1024]{3,2,1,0:T(8,128)} %fusion.12, f32[5,4,192,1024]{3,2,1,0:T(8,128)S(1)} %copy-done.1, f32[3,4,192,1024]{3,2,1,0:T(8,128)} %param.2, f32[3,4,192,1024]{3,2,1,0:T(8,128)} %param.3), kind=kLoop, calls=%fused_computation.71 | loop fusion | flops 18874368 | bytes 40894464 | tf_op jit(solution)/shard_map/sub | solution.py:74
  491.9 56.7 %all-to-all-done.1 = f32[2,5,4,192,512]{4,3,2,1,0:T(8,128)} async-done(((f32[2,5,4,192,512]{4,3,2,1,0:T(8,128)}), f32[2,5,4,192,512]{4,3,2,1,0:T(8,128)}, u32[]{:S(2)}, u32[]{:S(2)}) %all-to-all-start.1) | async-done | bytes 15728672 | tf_op jit(solution)/shard_map/all_to_all | solution.py:16
  548.6 11.9 %slice_bitcast_fusion.6 = (f32[2,1,4,24,8,512]{5,4,3,2,1,0:T(8,128)}, f32[2,1,4,24,8,512]{5,4,3,2,1,0:T(8,128)}, f32[2,1,4,24,8,512]{5,4,3,2,1,0:T(8,128)}, f32[...) fusion(f32[5,4,192,2,512]{4,2,1,0,3:T(8,128)} %bitcast.8), kind=kLoop, calls=%fused_computation.56 | loop fusion | bytes 31457280
  560.5 0.0 copy-start.4
  560.5 2.4 copy.18
  562.9 0.0 copy-start.3
  562.9 0.0 slice-start
  562.9 2.4 copy.19
  565.3 0.0 slice-start.1
  565.4 0.4 copy.20
  565.7 0.0 copy-done.4
  565.7 0.0 slice-start.2
  565.7 0.4 copy.21
  566.1 0.0 copy-done.3
  566.1 2.0 copy.22
  568.1 0.0 slice-done
  568.1 1.4 slice-done.1
  569.5 0.2 slice-done.2
  569.8 0.0 copy-start.5
  569.8 8.3 %multiply_add_fusion.2 = (f32[1,4,192,1024]{3,2,1,0:T(8,128)}, f32[1,4,192,1024]{3,2,1,0:T(8,128)}, f32[1,4,192,1024]{3,2,1,0:T(8,128)}) fusion(f32[1,4,192,1024]{3,2,1,0:T(8,128)S(1)} %bitcast.36, f32[1,4,192,1024]{3,2,1,0:T(8,128)S(1)} %bitcast.35, f32[3,4,192,1024]{3,2,1,0:T(8,128)S(1)} %bitcast.33, f32[3,4,192,1024]{3,2,1,0:T(8,128)} %param.3, ...), kind=kLoop, calls=%fused_computation.75 | loop fusion | flops 11010048 | bytes 34603008 | tf_op jit(solution)/shard_map/add | solution.py:63
  578.1 0.0 copy-done.5
  578.1 11.9 %fusion.26 = f32[3,4,192,1024]{3,2,1,0:T(8,128)} fusion(f32[3,4,192,1024]{3,2,1,0:T(8,128)S(1)} %bitcast.33, f32[1,4,192,1024]{3,2,1,0:T(8,128)} %get-tuple-element.6, f32[1,4,192,1024]{3,2,1,0:T(8,128)} %fusion.33, f32[1,4,192,1024]{3,2,1,0:T(8,128)} %get-tuple-element.5, f32[1,4,192,1024]{3,2,1,0:T(8,128)} %get-tuple-element.9, ...), kind=kLoop, calls=%fused_computation.48 | loop fusion | flops 16515072 | bytes 37749504 | tf_op jit(solution)/shard_map/add | solution.py:122
  (3 shorter events, 0.0 us)
Async XLA Ops:
  0.0 5.5 copy-start
  5.5 7.4 %copy-start.2 = (f32[2,4,192,1024]{3,2,1,0:T(8,128)}, f32[2,4,192,1024]{3,2,1,0:T(8,128)S(1)}, u32[]{:S(2)}) copy-start(f32[2,4,192,1024]{3,2,1,0:T(8,128)S(1)} %slice.149) | copy-start | bytes 18874372
  12.9 364.4 %collective-permute-start = (f32[5,4,192,1024]{3,2,1,0:T(8,128)}, f32[5,4,192,1024]{3,2,1,0:T(8,128)}, u32[]{:S(2)}, u32[]{:S(2)}) collective-permute-start(f32[5,4,192,1024]{3,2,1,0:T(8,128)} %pad_maximum_fusion.1), channel_id=1, source_target_pairs={{2,0},{4,2},{6,4},{8,6},{10,8},{12,10},{14,12},{16,14},{18,16},{20... | collective-permute-start | bytes 47185928 | tf_op jit(solution)/shard_map/ppermute | solution.py:28
  13.7 363.6 %collective-permute-start.1 = (f32[5,4,192,1024]{3,2,1,0:T(8,128)}, f32[5,4,192,1024]{3,2,1,0:T(8,128)}, u32[]{:S(2)}, u32[]{:S(2)}) collective-permute-start(f32[5,4,192,1024]{3,2,1,0:T(8,128)} %pad_maximum_fusion.1), channel_id=1, source_target_pairs={{0,2},{2,4},{4,6},{6,8},{8,10},{10,12},{12,14},{14,16},{16,18},{18... | collective-permute-start | bytes 47185928 | tf_op jit(solution)/shard_map/ppermute | solution.py:27
  35.5 239.6 %all-to-all-start = ((f32[5,4,192,1024]{2,1,0,3:T(4,128)}), f32[5,4,192,1024]{2,1,0,3:T(4,128)}, u32[]{:S(2)}, u32[]{:S(2)}) async-start(f32[5,4,192,1024]{2,1,0,3:T(4,128)} %copy.10), calls=%async_computation | async-start | bytes 41943040 | tf_op jit(solution)/shard_map/all_to_all | solution.py:110
  367.8 180.8 %all-to-all-start.1 = ((f32[2,5,4,192,512]{4,3,2,1,0:T(8,128)}), f32[2,5,4,192,512]{4,3,2,1,0:T(8,128)}, u32[]{:S(2)}, u32[]{:S(2)}) async-start(f32[2,5,4,192,512]{4,3,2,1,0:T(8,128)} %pad_maximum_fusion.2), calls=%async_computation.1 | async-start | bytes 31457280 | tf_op jit(solution)/shard_map/all_to_all | solution.py:16
  465.8 14.7 %copy-start.1 = (f32[5,4,192,1024]{3,2,1,0:T(8,128)S(1)}, f32[5,4,192,1024]{3,2,1,0:T(8,128)}, u32[]{:S(2)}) copy-start(f32[5,4,192,1024]{3,2,1,0:T(8,128)} %fusion.3) | copy-start | bytes 47185924
  560.5 5.2 copy-start.4
  562.9 3.2 copy-start.3
  562.9 5.2 slice-start
  565.3 4.2 slice-start.1
  565.7 4.0 slice-start.2
  569.8 8.3 %copy-start.5 = (f32[192]{0:T(256)S(1)}, f32[192]{0:T(256)}, u32[]{:S(2)}) copy-start(f32[192]{0:T(256)} %add_multiply_fusion) | copy-start | bytes 2308
